TPU v7x, 256 devices: a whole 4x4x8 slice. The times are simulated.
256 devices in a mesh: grp: 2 (over core), ep: 128 (over y, x, z).
Axes of the slice: x: 4, y: 4, z: 8, core: 2. Of those that a mesh axis runs over, the one named last changes fastest.
Arguments:
- hidden: bfloat16 [2, 32768, 2048], P('grp', 'ep'), may hold values from -6 to 6
- norm_gain: float32 [2, 2048], P('grp'), may hold values from 0.1 to 1.9
- final_gain: float32 [2, 2048], P('grp'), may hold values from 0.1 to 1.9
- router: bfloat16 [2, 2048, 128], P('grp'), may hold values from -0.125 to 0.125
- w_in: bfloat16 [2, 2048, 131072], P('grp', None, 'ep'), may hold values from -0.125 to 0.125
- w_out: bfloat16 [2, 131072, 2048], P('grp', 'ep'), may hold values from -0.375 to 0.375
- expert_ids: int32 [2, 32768, 2], P('grp', 'ep'), may hold values from 0 to 127, as said below
- slot_ids: int32 [2, 32768, 2], P('grp', 'ep'), may hold values from -1 to 5, as said below
- src_len: int32 [128, 4], P('ep'), may hold values from 1 to 128, 256 in all within a row
- tgt_len: int32 [128, 4], P('ep'), may hold values from 1 to 85, 171 in all within a row
- wq: bfloat16 [2048, 1024], P('ep'), may hold values from -1 to 1
- wk: bfloat16 [2048, 1024], P('ep'), may hold values from -1 to 1
- wv: bfloat16 [2048, 1024], P('ep'), may hold values from -0.125 to 0.125
- wo: bfloat16 [2048, 1024], P('ep'), may hold values from -0.5 to 0.5
Outputs:
- layer_out: bfloat16 [2, 32768, 2048], P('grp', 'ep')
Inputs may be any that keep to these rules, and one draw needn't show every extreme that they name: `expert_ids`: each row names two different experts; at most one of them is below 16. `slot_ids`: -1 where the expert is 16 or more; otherwise a slot that no other route of the same device block to the same expert takes. In each group one expert gets all 6 slots from every device block.
All inputs are finite; a program needn't handle non-finite values.
Results may differ from a plain program's by a relative error of at most 0.02.
The roundings to bfloat16 on the way count: a program that leaves them out, or rounds other values in their place, can miss the bound.
Values may be sent and summed in bfloat16 or wider, within the bound.
A program may use at most 128 MiB of HBM per device.

v0:
```python
import jax
import jax.numpy as jnp
from jax import lax
from jax.sharding import PartitionSpec as P

HD = 128
SPLIT = 8
C = 6
SENT = 4


def shifted(value, axis, steps):
    count = lax.axis_size(axis)
    first, last = (max(0, -steps), min(count, count - steps))
    return lax.ppermute(value, axis, [(source, source + steps) for source in range(first, last)])


def normalize(values, gain):
    mean = jnp.mean(values, -1, keepdims=True)
    centred = values - mean
    spread = jnp.mean(centred * centred, -1, keepdims=True)
    return centred * lax.rsqrt(spread + 1e-05) * gain


def positions(lengths, count):
    ends = jnp.cumsum(lengths)
    above = (jnp.arange(count, dtype=jnp.int32)[:, None] >= ends[None, :]).astype(jnp.int32)
    return jnp.sum(above, axis=1)


def body(
    hidden,
    norm_gain,
    final_gain,
    router,
    w_in,
    w_out,
    expert_ids,
    slot_ids,
    src_len,
    tgt_len,
    wq,
    wk,
    wv,
    wo,
):
    devices = lax.axis_size("ep")
    experts_here = devices // SPLIT
    rows_here = hidden.shape[1]
    width = hidden.shape[2]
    resid = hidden[0].astype(jnp.float32)
    normed = normalize(resid, norm_gain[0]).astype(jnp.bfloat16)
    logits = jnp.dot(normed, router[0], preferred_element_type=jnp.float32)
    routes = expert_ids[0]
    slots = slot_ids[0]
    picked = jnp.take_along_axis(logits, routes, axis=1)
    gate = jax.nn.sigmoid(picked - picked[:, ::-1])
    live = slots >= 0
    place = jnp.max(jnp.where(live, routes * C + slots, -1), axis=1)
    weight = jnp.sum(jnp.where(live, gate, 0.0), axis=1)
    table = (jnp.arange(experts_here * C)[:, None] == place[None, :]).astype(jnp.bfloat16)
    packed = jnp.dot(table, normed, preferred_element_type=jnp.float32).astype(jnp.bfloat16)
    outgoing = jnp.broadcast_to(
        packed.reshape(experts_here, 1, C, width), (experts_here, SPLIT, C, width)
    )
    outgoing = outgoing.reshape(devices, C, width)
    arrived = lax.all_to_all(outgoing, "ep", split_axis=0, concat_axis=0, tiled=True)
    flat = arrived.reshape(-1, width)
    inner = jax.nn.relu(jnp.dot(flat, w_in[0], preferred_element_type=jnp.float32)).astype(
        jnp.bfloat16
    )
    partial_out = jnp.dot(inner, w_out[0], preferred_element_type=jnp.float32).astype(jnp.bfloat16)
    back = lax.all_to_all(
        partial_out.reshape(arrived.shape), "ep", split_axis=0, concat_axis=0, tiled=True
    )
    summed = jnp.sum(back.reshape(experts_here, SPLIT, C, width).astype(jnp.float32), axis=1)
    summed = summed.reshape(experts_here * C, width)
    moe_term = jnp.take(summed, jnp.maximum(place, 0), axis=0) * weight[:, None]
    mixed = resid + moe_term
    normed_out = normalize(mixed, final_gain[0]).astype(jnp.bfloat16)
    group = lax.axis_index("grp")
    heads_width = wq.shape[1]
    memory = shifted(normed_out, "grp", 1)
    q_total = jnp.dot(
        normed_out, lax.all_gather(wq, "ep", axis=0, tiled=True), preferred_element_type=jnp.float32
    )
    k_total = jnp.dot(
        memory, lax.all_gather(wk, "ep", axis=0, tiled=True), preferred_element_type=jnp.float32
    )
    v_total = jnp.dot(
        memory, lax.all_gather(wv, "ep", axis=0, tiled=True), preferred_element_type=jnp.float32
    )
    query = q_total.astype(jnp.bfloat16)
    keys = k_total.astype(jnp.bfloat16)
    values = v_total.astype(jnp.bfloat16)
    seg_q = positions(tgt_len[0], rows_here)
    seg_k = positions(src_len[0], rows_here)
    valid = seg_q < SENT
    allowed = (seg_q[:, None] == seg_k[None, :]) & valid[:, None]
    heads = heads_width // HD
    scores = jnp.einsum(
        "qhd,khd->hqk",
        query.reshape(rows_here, heads, HD),
        keys.reshape(rows_here, heads, HD),
        preferred_element_type=jnp.float32,
    ) * HD ** (-0.5)
    scores = jnp.where(allowed[None], scores, -1e30)
    top = jnp.max(scores, axis=-1, keepdims=True)
    expd = jnp.exp(scores - top)
    prob = (expd / jnp.sum(expd, axis=-1, keepdims=True)).astype(jnp.bfloat16)
    context = jnp.einsum(
        "hqk,khd->qhd",
        prob,
        values.reshape(rows_here, heads, HD),
        preferred_element_type=jnp.float32,
    )
    context = context.astype(jnp.bfloat16).reshape(rows_here, heads_width)
    attended = lax.dot_general(
        context,
        lax.all_gather(wo, "ep", axis=0, tiled=True),
        (((1,), (1,)), ((), ())),
        preferred_element_type=jnp.float32,
    )
    attended = jnp.where(valid[:, None], attended, 0.0)
    decoded = (mixed + attended).astype(jnp.bfloat16)
    return jnp.where(group == 0, normed_out, decoded)[None]


def solution(mesh):
    in_specs = (
        P("grp", "ep", None),
        P("grp", None),
        P("grp", None),
        P("grp", None, None),
        P("grp", None, "ep"),
        P("grp", "ep", None),
        P("grp", "ep", None),
        P("grp", "ep", None),
        P("ep", None),
        P("ep", None),
        P("ep", None),
        P("ep", None),
        P("ep", None),
        P("ep", None),
    )
    out_specs = P("grp", "ep", None)
    return jax.shard_map(body, mesh=mesh, in_specs=in_specs, out_specs=out_specs, check_vma=False)
```

profile of v0, /device:TPU:1, one launch (start us, length us, event | category | flops | bytes accessed | tf_op | source)
XLA Modules:
  0.0 527.9 jit_solution(986029167325764737)
XLA Ops:
  6.5 0.0 copy-start
  6.5 0.0 all-gather.7.cloned.1.call-start
  6.5 0.7 all-gather.7.cloned.1.call-update
  7.3 0.0 all-gather.5.cloned.1.call-start
  7.3 0.7 all-gather.5.cloned.1.call-update
  8.0 0.8 copy.26
  8.8 0.8 copy.27
  9.7 0.1 fusion.48
  9.8 1.4 convert_reduce_fusion.1
  11.2 0.0 copy-done.2
  11.2 0.4 fusion.16
  11.7 0.0 copy-done.6
  11.7 0.6 convolution_convert_fusion
  12.2 0.1 broadcast_in_dim.76
  12.4 2.5 broadcast_in_dim.77
  14.8 16.9 %all-to-all-start = ((bf16[128,6,2048]{2,1,0:T(8,128)(2,1)}), bf16[128,6,2048]{2,1,0:T(8,128)(2,1)}, u32[]{:S(2)}, u32[]{:S(2)}) async-start(bf16[128,6,2048]{2,1,0:T(8,128)(2,1)} %bitcast.111), calls=%async_computation | async-start | bytes 8388608 | tf_op jit(solution)/shard_map/all_to_all | solution.py:67
  31.7 0.0 all-gather.9.cloned.1.call-start
  31.8 0.7 all-gather.9.cloned.1.call-update
  32.5 106.2 %all-to-all-done = bf16[128,6,2048]{2,1,0:T(8,128)(2,1)} async-done(((bf16[128,6,2048]{2,1,0:T(8,128)(2,1)}), bf16[128,6,2048]{2,1,0:T(8,128)(2,1)}, u32[]{:S(2)}, u32[]{:S(2)}) %all-to-all-start) | async-done | bytes 3145760 | tf_op jit(solution)/shard_map/all_to_all | solution.py:67
  138.6 6.3 %reshape.221 = bf16[768,2048]{1,0:T(8,128)(2,1)} reshape(bf16[128,6,2048]{2,1,0:T(8,128)(2,1)} %all-to-all-done) | data formatting | bytes 6291456 | tf_op jit(solution)/shard_map/reshape | solution.py:68
  145.0 6.7 %maximum_convert_fusion = bf16[768,1024]{1,0:T(8,128)(2,1)S(1)} fusion(bf16[768,2048]{1,0:T(8,128)(2,1)} %reshape.221, bf16[1,2048,1024]{2,1,0:T(8,128)(2,1)} %param.18), kind=kOutput, calls=%fused_computation.9 | convolution fusion | flops 3222798336 | bytes 8912896 | tf_op jit(solution)/shard_map/dot_general | solution.py:69
  151.7 0.0 copy-done.5
  151.7 4.8 fusion.5
  156.4 6.2 %reshape.222 = bf16[128,6,2048]{2,1,0:T(8,128)(2,1)} reshape(bf16[768,2048]{1,0:T(8,128)(2,1)} %fusion.5) | data formatting | bytes 6291456 | tf_op jit(solution)/shard_map/reshape | solution.py:74
  162.7 7.5 %all-to-all-start.1 = ((bf16[128,6,2048]{2,1,0:T(8,128)(2,1)}), bf16[128,6,2048]{2,1,0:T(8,128)(2,1)}, u32[]{:S(2)}, u32[]{:S(2)}) async-start(bf16[128,6,2048]{2,1,0:T(8,128)(2,1)} %reshape.222), calls=%async_computation.1 | async-start | bytes 8388608 | tf_op jit(solution)/shard_map/all_to_all | solution.py:73
  170.2 0.2 all-gather.11.cloned.1.call-start
  170.5 0.3 all-gather.11.cloned.1.call-update
  170.8 0.0 copy-done.4
  170.8 0.1 copy.28
  171.0 0.1 reshape.241
  171.1 0.6 fusion.28
  171.7 0.0 copy-start.7
  171.7 3.6 gather_fusion.1
  175.3 0.1 reshape.244
  175.5 0.2 rev.3
  175.7 0.0 copy-done.7
  175.7 0.2 reduce-window.16
  175.9 0.1 fusion.50
  176.1 98.5 %all-to-all-done.1 = bf16[128,6,2048]{2,1,0:T(8,128)(2,1)} async-done(((bf16[128,6,2048]{2,1,0:T(8,128)(2,1)}), bf16[128,6,2048]{2,1,0:T(8,128)(2,1)}, u32[]{:S(2)}, u32[]{:S(2)}) %all-to-all-start.1) | async-done | bytes 3145760 | tf_op jit(solution)/shard_map/all_to_all | solution.py:73
  274.5 3.4 convert_reduce_fusion
  277.9 0.1 reshape.223
  278.0 2.7 gather_fusion
  280.7 2.3 fusion.69
  283.1 0.0 copy-start.3
  283.1 0.3 multiply_reduce_fusion
  283.4 0.0 copy-start.8
  283.5 0.3 copy-done.3
  283.8 1.3 multiply_convert_fusion
  285.1 1.3 collective-permute-start
  286.4 0.1 convert_reduce_fusion.3
  286.5 0.2 reduce-window.17
  286.7 0.1 convert_reduce_fusion.2
  286.8 0.1 compare_and_fusion
  286.9 0.0 all-gather.7.cloned.1.call-done
  286.9 4.6 fusion.25
  291.5 7.0 %collective-permute-done = bf16[256,2048]{1,0:T(8,128)(2,1)} collective-permute-done((bf16[256,2048]{1,0:T(8,128)(2,1)}, bf16[256,2048]{1,0:T(8,128)(2,1)}, u32[]{:S(2)}, u32[]{:S(2)}) %collective-permute-start) | collective-permute-done | bytes 1048608 | tf_op jit(solution)/shard_map/ppermute | solution.py:15
  298.5 3.8 convolution_convert_fusion.4
  302.3 0.2 copy.34
  302.5 96.6 %all-gather.9.cloned.1.call-done = bf16[2048,1024]{1,0:T(8,128)(2,1)} async-done(((bf16[16,1024]{1,0:T(8,128)(2,1)}), bf16[2048,1024]{1,0:T(8,128)(2,1)}) %all-gather.9.cloned.1.call-update) | async-done | bytes 4194320 | tf_op jit(solution)/shard_map/all_gather | solution.py:88
  399.2 4.6 fusion.26
  403.7 3.2 fusion.71
  407.0 1.9 convolution_convert_fusion.1
  408.9 107.8 %all-gather.11.cloned.1.call-done = bf16[2048,1024]{1,0:T(8,128)(2,1)} async-done(((bf16[16,1024]{1,0:T(8,128)(2,1)}), bf16[2048,1024]{1,0:T(8,128)(2,1)}) %all-gather.11.cloned.1.call-update) | async-done | bytes 4194320 | tf_op jit(solution)/shard_map/all_gather | solution.py:120
  516.7 4.7 fusion.15
  (21 shorter events, 0.1 us)
Async XLA Ops:
  6.5 164.6 %copy-start = (bf16[1,2048,128]{2,1,0:T(8,128)(2,1)S(1)}, bf16[1,2048,128]{2,1,0:T(8,128)(2,1)}, u32[]{:S(2)}) copy-start(bf16[1,2048,128]{2,1,0:T(8,128)(2,1)} %param.17) | copy-start | bytes 1572868
  6.5 4.7 copy-start.2
  6.5 5.1 copy-start.6
  6.5 280.4 %all-gather.7.cloned.1.call-start = ((), (), s32[]{:S(2)}) async-start(), calls=%async_computation.3 | async-start | bytes 4227072 | tf_op jit(solution)/shard_map/all_gather | solution.py:85
  7.3 284.2 %all-gather.5.cloned.1.call-start = ((), (), s32[]{:S(2)}) async-start(), calls=%async_computation.2 | async-start | bytes 4227072 | tf_op jit(solution)/shard_map/all_gather | solution.py:91
  14.8 123.8 %all-to-all-start = ((bf16[128,6,2048]{2,1,0:T(8,128)(2,1)}), bf16[128,6,2048]{2,1,0:T(8,128)(2,1)}, u32[]{:S(2)}, u32[]{:S(2)}) async-start(bf16[128,6,2048]{2,1,0:T(8,128)(2,1)} %bitcast.111), calls=%async_computation | async-start | bytes 8388608 | tf_op jit(solution)/shard_map/all_to_all | solution.py:67
  31.7 367.5 %all-gather.9.cloned.1.call-start = ((), (), s32[]{:S(2)}) async-start(), calls=%async_computation.4 | async-start | bytes 4227072 | tf_op jit(solution)/shard_map/all_gather | solution.py:88
  145.0 6.7 %copy-start.5 = (bf16[1,1024,2048]{2,1,0:T(8,128)(2,1)S(1)}, bf16[1,1024,2048]{2,1,0:T(8,128)(2,1)}, u32[]{:S(2)}) copy-start(bf16[1,1024,2048]{2,1,0:T(8,128)(2,1)} %param.19) | copy-start | bytes 12582916
  162.7 8.1 %copy-start.4 = (s32[1,256,2]{1,2,0:T(2,128)S(1)}, s32[1,256,2]{1,2,0:T(2,128)}, u32[]{:S(2)}) copy-start(s32[1,256,2]{1,2,0:T(2,128)} %param.20) | copy-start | bytes 6148
  162.7 111.8 %all-to-all-start.1 = ((bf16[128,6,2048]{2,1,0:T(8,128)(2,1)}), bf16[128,6,2048]{2,1,0:T(8,128)(2,1)}, u32[]{:S(2)}, u32[]{:S(2)}) async-start(bf16[128,6,2048]{2,1,0:T(8,128)(2,1)} %reshape.222), calls=%async_computation.1 | async-start | bytes 8388608 | tf_op jit(solution)/shard_map/all_to_all | solution.py:73
  170.2 346.4 %all-gather.11.cloned.1.call-start = ((), (), s32[]{:S(2)}) async-start(), calls=%async_computation.5 | async-start | bytes 4227072 | tf_op jit(solution)/shard_map/all_gather | solution.py:120
  171.7 4.0 copy-start.7
  283.1 0.7 copy-start.3
  283.4 3.0 copy-start.8
  285.1 13.4 %collective-permute-start = (bf16[256,2048]{1,0:T(8,128)(2,1)}, bf16[256,2048]{1,0:T(8,128)(2,1)}, u32[]{:S(2)}, u32[]{:S(2)}) collective-permute-start(bf16[256,2048]{1,0:T(8,128)(2,1)} %multiply_convert_fusion), channel_id=1, source_target_pairs={{0,128},{1,129},{2,130},{3,131},{4,132},{5,133},{6,134},{7,135},{8... | collective-permute-start | bytes 3145736 | tf_op jit(solution)/shard_map/ppermute | solution.py:15
  302.5 101.2 %copy-start.9 = (bf16[32,8,8,128]{3,2,1,0:T(8,128)(2,1)S(1)}, bf16[32,8,8,128]{3,2,1,0:T(8,128)(2,1)}, u32[]{:S(2)}) copy-start(bf16[32,8,8,128]{3,2,1,0:T(8,128)(2,1)} %fusion.25) | copy-start | bytes 1572868
  516.7 4.7 copy-start.1
Sparse Core Ops, SparseCore 0:
  11.0 134.5 all-gather.6
  149.2 132.8 all-gather.4
  285.7 113.4 all-gather.8
  402.7 113.9 all-gather.10
where the time goes:
time: 532 us; the launch traced here: 528 us
  waiting for transfers between devices  419 us (79%)
  matrix products  35.4 us (7%)
  starting transfers between devices  26 us (5%)
  local copies, waits for them, and re-layouts  24.4 us (5%)
  between operations  13.4 us (3%)
  other arithmetic  10.2 us (2%)
    all_gather x1, waiting for transfers between devices, body(): lax.all_gather(wo, 'ep', axis=0, tiled=True)  108 us
    all_to_all x1, waiting for transfers between devices, body(): lax.all_to_all(outgoing, 'ep', split_axis=0, concat_axis=0, tiled=True)  106 us
    all_to_all x1, waiting for transfers between devices, body(): lax.all_to_all(partial_out.reshape(arrived.shape), 'ep', split_axis=0, co...  98.5 us
    all_gather x1, waiting for transfers between devices, body(): lax.all_gather(wk, 'ep', axis=0, tiled=True)  96.6 us
    all_to_all x1, starting transfers between devices, body(): lax.all_to_all(outgoing, 'ep', split_axis=0, concat_axis=0, tiled=True)  16.9 us
  transfers between devices with their start and end apart: 7, of which 5 were waited for; matrix products, arithmetic and copies ran while one was open for 12% of the time, Pallas kernels for 0%

commit v1 on v0

v1 whole, which is shorter than its diff:
```python
import jax
import jax.numpy as jnp
from jax import lax
from jax.experimental import pallas as pl
from jax.experimental.pallas import tpu as pltpu
from jax.sharding import PartitionSpec as P

NY, NX, NZ = 4, 4, 8
E = NY * NX
C = 6
HALF = E // 2 * C
SENT = 4
HD = 128
ROWS_Q = 176
F32 = jnp.float32
BF16 = jnp.bfloat16

UP_ORDER = [(0, 1), (1, 1), (0, 2), (1, 2), (0, 3), (1, 3), (0, 4)]
DOWN_ORDER = [(1, 1), (0, 1), (1, 2), (0, 2), (1, 3), (0, 3), (1, 4)]
BACK_DOWN = [(1, 3), (0, 4), (1, 2), (0, 3), (1, 1), (0, 2), (0, 1)]
BACK_UP = [(0, 3), (1, 4), (0, 2), (1, 3), (0, 1), (1, 2), (1, 1)]
FAR_DOWN = (4, 3)
FAR_UP = (3, 4)


def back_slot(far, half, k):
    return (far[0] if half else 0) + k


def norm_rows(v, gain):
    mean = jnp.mean(v, -1, keepdims=True)
    centred = v - mean
    spread = jnp.mean(centred * centred, -1, keepdims=True)
    return centred * lax.rsqrt(spread + 1e-05) * gain


def kernel(
    hidden_hbm, norm_gain, final_gain, router_hbm, w_in_hbm, w_out_hbm, ids_ref, slots_ref, src_ref, tgt_ref,
    wq_ref, wk_ref, wv_ref, wo_ref,
    out_ref,
    hid, normed, router, w_in, w_out, packed, arrived, tokens, partial, sums, inner, total, returning, returned,
    mixed, weights, kv_out, kv_in, query, context, gate_ref, place_ref,
    load_sem, pack_send, pack_recv, ring_send, ring_recv, back_send, back_recv, wz_send, wz_recv,
    wxy_send, wxy_recv, ret_send, ret_recv, kv_send, kv_recv,
):
    rows, width = hid.shape
    hw = width // 2
    ep = lax.axis_index("ep")
    grp = lax.axis_index("grp")
    z = lax.rem(ep, NZ)
    e = ep // NZ
    x = lax.rem(e, NX)
    y = e // NX

    def at(yy, xx, zz):
        return (yy * NX + xx) * NZ + zz

    def zmod(v):
        return lax.rem(v + NZ, NZ)

    def xmod(v):
        return lax.rem(v + NX, NX)

    def remote(src, dst, send, recv, target):
        return pltpu.make_async_remote_copy(
            src_ref=src, dst_ref=dst, send_sem=send, recv_sem=recv,
            device_id={"ep": target}, device_id_type=pl.DeviceIdType.MESH,
        )

    sent = []

    def send(*args):
        copy = remote(*args)
        copy.start()
        sent.append(copy)

    def landed(dst, recv):
        remote(dst, dst, kv_send.at[0], recv, ep).wait_recv()

    z_up, z_down = at(y, x, zmod(z + 1)), at(y, x, zmod(z - 1))
    peers = []
    for dy in (2, 1, 3, 0):
        for dx in (2, 1, 3, 0):
            if dy or dx:
                peers.append((xmod(y + dy), xmod(x + dx)))

    loads = [
        pltpu.make_async_copy(hidden_hbm, hid, load_sem.at[0]),
        pltpu.make_async_copy(router_hbm, router, load_sem.at[1]),
        pltpu.make_async_copy(w_in_hbm, w_in, load_sem.at[2]),
        pltpu.make_async_copy(w_out_hbm, w_out, load_sem.at[3]),
    ]
    loads[0].start()
    barrier = pltpu.get_barrier_semaphore()
    for target in [at(yy, xx, z) for yy, xx in peers] + [z_up, z_down]:
        pl.semaphore_signal(barrier, inc=1, device_id={"ep": target}, device_id_type=pl.DeviceIdType.MESH)
    pl.semaphore_signal(barrier, inc=1, device_id={"grp": 1 - grp}, device_id_type=pl.DeviceIdType.MESH)
    for copy in loads[1:]:
        copy.start()

    first = grp == 0
    weights[0, e, z] = jnp.where(first, wk_ref[...], wq_ref[...])
    weights[1, e, z] = jnp.where(first, wv_ref[...], wo_ref[...])

    ids_row = ids_ref[...]
    slots_row = slots_ref[...]
    place_row = jnp.max(jnp.where(slots_row >= 0, ids_row * 16 + slots_row, -1000), axis=0, keepdims=True)
    stacked = jnp.concatenate([ids_row, slots_row, jnp.broadcast_to(place_row, (4, rows))], axis=0)
    columns = jnp.transpose(stacked.astype(F32)).astype(jnp.int32)
    ids, live = columns[:, 0:2], columns[:, 2:4] >= 0
    place_ref[...] = columns[:, 4:5]

    loads[0].wait()

    def norm_in(i, carry):
        at_rows = pl.ds(pl.multiple_of(i * 32, 32), 32)
        normed[at_rows, :] = norm_rows(hid[at_rows, :].astype(F32), norm_gain[...]).astype(BF16)
        return carry

    lax.fori_loop(0, rows // 32, norm_in, 0)

    slot_iota = lax.broadcasted_iota(jnp.int32, (E * 16, rows), 0)
    pick0 = (slot_iota == place_row).astype(F32).astype(BF16)
    pick1 = (slot_iota == place_row + 8).astype(F32).astype(BF16)
    for j in range(hw // 256):
        c0, c1 = j * 256, hw + j * 256
        got = jnp.dot(pick0, normed[:, c0:c0 + 256], preferred_element_type=F32) + jnp.dot(
            pick1, normed[:, c1:c1 + 256], preferred_element_type=F32
        )
        packed[:, :, c0:c0 + 256] = got.astype(BF16).reshape(E, 16, 256)

    pl.semaphore_wait(barrier, len(peers) + 3)

    for i, (yy, xx) in enumerate(peers):
        peer = yy * NX + xx
        send(packed.at[peer], arrived.at[e], pack_send.at[i], pack_recv.at[e], peer * NZ + z)
    own = pltpu.make_async_copy(packed.at[e], arrived.at[e], load_sem.at[4])
    own.start()

    def wz_hop(slot):
        for way, (order, sign, target) in enumerate(((UP_ORDER, 1, z_up), (DOWN_ORDER, -1, z_down))):
            half, k = order[slot]
            block = zmod(z - sign * (k - 1))
            ref = weights.at[half, e, block]
            send(ref, ref, wz_send.at[way, slot], wz_recv.at[way, slot], target)

    def wz_wait(slot):
        for way, (order, sign) in enumerate(((UP_ORDER, 1), (DOWN_ORDER, -1))):
            half, k = order[slot]
            ref = weights.at[half, e, zmod(z - sign * k)]
            landed(ref, wz_recv.at[way, slot])

    wz_hop(0)
    wz_hop(1)

    loads[1].wait()
    logits = jnp.dot(normed[...], router[...], preferred_element_type=F32)
    lane = lax.broadcasted_iota(jnp.int32, logits.shape, 1)
    pick_a = jnp.sum(jnp.where(lane == ids[:, 0:1], logits, 0.0), axis=1, keepdims=True)
    pick_b = jnp.sum(jnp.where(lane == ids[:, 1:2], logits, 0.0), axis=1, keepdims=True)
    gate_ref[...] = jnp.where(live[:, 0:1], jax.nn.sigmoid(pick_a - pick_b), 0.0) + jnp.where(
        live[:, 1:2], jax.nn.sigmoid(pick_b - pick_a), 0.0
    )

    for slot in range(5):
        wz_wait(slot)
        wz_hop(slot + 2)

    own.wait()
    for yy, xx in peers:
        peer = yy * NX + xx
        landed(arrived.at[peer], pack_recv.at[peer])
    r_iota = lax.broadcasted_iota(jnp.int32, (HALF, E * 8), 0)
    q_iota = lax.broadcasted_iota(jnp.int32, (HALF, E * 8), 1)
    base = (r_iota // C) * 16 + r_iota % C
    fold0 = (q_iota == base).astype(F32).astype(BF16)
    fold1 = (q_iota == base + 8).astype(F32).astype(BF16)
    for half in range(2):
        got = arrived[half * (E // 2):(half + 1) * (E // 2)].reshape(E * 8, hw)
        tokens[z, half, :, :hw] = jnp.dot(fold0, got, preferred_element_type=F32).astype(BF16)
        tokens[z, half, :, hw:] = jnp.dot(fold1, got, preferred_element_type=F32).astype(BF16)

    def ring_hop(slot):
        for way, (order, sign, target) in enumerate(((UP_ORDER, 1, z_up), (DOWN_ORDER, -1, z_down))):
            half, k = order[slot]
            ref = tokens.at[zmod(z - sign * (k - 1)), half]
            send(ref, ref, ring_send.at[way, slot], ring_recv.at[way, slot], target)

    def ring_wait(slot):
        for way, (order, sign) in enumerate(((UP_ORDER, 1), (DOWN_ORDER, -1))):
            half, k = order[slot]
            landed(tokens.at[zmod(z - sign * k), half], ring_recv.at[way, slot])

    def expert(block_a, half_a, block_b, half_b):
        def first_step(j, carry):
            cols = pl.ds(pl.multiple_of(j * 256, 256), 256)
            both = jnp.concatenate([tokens[block_a, half_a], tokens[block_b, half_b]], axis=0)
            got = jnp.dot(both, w_in[:, cols], preferred_element_type=F32)
            inner[:, cols] = jnp.maximum(got, 0.0).astype(BF16)
            return carry

        def second_step(j, carry):
            cols = pl.ds(pl.multiple_of(j * 256, 256), 256)
            got = jnp.dot(inner[...], w_out[:, cols], preferred_element_type=F32).astype(BF16)
            partial[block_a, half_a, :, cols] = got[:HALF]
            partial[block_b, half_b, :, cols] = got[HALF:]
            return carry

        lax.fori_loop(0, w_in.shape[1] // 256, first_step, 0)
        lax.fori_loop(0, width // 256, second_step, 0)

    def expert_slot(slot):
        (half_a, k), (half_b, _) = UP_ORDER[slot], DOWN_ORDER[slot]
        expert(zmod(z - k), half_a, zmod(z + k), half_b)

    def block_at(w, a, b):
        xx, yy = (xmod(x + a), xmod(y + b)) if w == 0 else (xmod(x + b), xmod(y + a))
        return yy * NX + xx

    def go(w, phase, sign):
        if (w == 0) == (phase == 0):
            return at(y, xmod(x + sign), z)
        return at(xmod(y + sign), x, z)

    w_count = [0]

    def wxy(w, a, b, part, phase, sign):
        blk = block_at(w, a, b)
        ref = weights.at[w, blk] if part is None else weights.at[w, blk, pl.ds(part * 4, 4)]
        send(ref, ref, wxy_send.at[w_count[0]], wxy_recv.at[w, blk, part or 0], go(w, phase, sign))
        w_count[0] += 1

    def wxy_wait(w, a, b):
        blk = block_at(w, a, b)
        opposite = b == 2 or (b == 0 and a == 2)
        if opposite:
            for part in range(2):
                landed(weights.at[w, blk, pl.ds(part * 4, 4)], wxy_recv.at[w, blk, part])
        else:
            landed(weights.at[w, blk], wxy_recv.at[w, blk, 0])

    def forward(w, a, b, phase):
        if phase == 0:
            wxy(w, a, b, 0 if a == 1 else 1, 0, -1 if a == 1 else 1)
        else:
            wxy(w, a, b, 0 if b == 1 else 1, 1, -1 if b == 1 else 1)

    def plane0():
        for w in range(2):
            for phase in range(2):
                for sign in (1, -1):
                    wxy(w, 0, 0, None, phase, sign)

    def plane1():
        for w in range(2):
            for a in (1, 3):
                wxy_wait(w, a, 0)
                forward(w, a, 0, 0)
        for w in range(2):
            for b in (1, 3):
                wxy_wait(w, 0, b)
                forward(w, 0, b, 1)
        for w in range(2):
            for a in (1, 3):
                for sign in (1, -1):
                    wxy(w, a, 0, None, 1, sign)

    def plane2():
        for w in range(2):
            wxy_wait(w, 2, 0)
            for sign in (1, -1):
                wxy(w, 2, 0, None, 1, sign)
        for w in range(2):
            for a in (1, 3):
                for b in (1, 3):
                    wxy_wait(w, a, b)
                    forward(w, a, b, 1)

    def plane3():
        for w in range(2):
            for b in (1, 3):
                wxy_wait(w, 2, b)
                forward(w, 2, b, 1)

    def plane4(w):
        for a in range(4):
            wxy_wait(w, a, 2)

    ring_hop(0)
    ring_hop(1)
    wz_wait(5)
    wz_wait(6)
    plane0()
    loads[2].wait()
    loads[3].wait()
    expert(z, 0, z, 1)
    for slot in range(5):
        ring_wait(slot)
        ring_hop(slot + 2)
        expert_slot(slot)
        if slot == 2:
            plane1()

    def back_add(way, step):
        order, far, sign = ((BACK_DOWN, FAR_DOWN, 1), (BACK_UP, FAR_UP, -1))[way]
        half, k = order[step]
        if k < far[half]:
            slot = back_slot(far, half, k)
            landed(sums.at[way, slot], back_recv.at[way, slot])
            block = zmod(z - sign * k)
            partial[block, half] = (
                partial[block, half].astype(F32) + sums[way, slot].astype(F32)
            ).astype(BF16)

    def back_send_step(way, step):
        order, far, sign = ((BACK_DOWN, FAR_DOWN, 1), (BACK_UP, FAR_UP, -1))[way]
        half, k = order[step]
        slot = back_slot(far, half, k - 1)
        send(
            partial.at[zmod(z - sign * k), half], sums.at[way, slot], back_send.at[way, step],
            back_recv.at[way, slot], (z_down, z_up)[way],
        )

    ring_wait(5)
    expert_slot(5)
    for way in range(2):
        back_send_step(way, 0)
    ring_wait(6)
    expert_slot(6)
    for step in range(1, 7):
        for way in range(2):
            back_add(way, step)
            back_send_step(way, step)
        if step == 1:
            plane2()
        if step == 4:
            plane3()

    q_iota = lax.broadcasted_iota(jnp.int32, (E * 8, HALF), 0)
    r_iota = lax.broadcasted_iota(jnp.int32, (E * 8, HALF), 1)
    c_iota = q_iota % 8
    source = jnp.where(c_iota < C, (q_iota // 16) * C + c_iota, -1)
    low = (q_iota // 8) % 2 == 0
    unfold0 = ((r_iota == source) & low).astype(F32).astype(BF16)
    unfold1 = ((r_iota == source) & jnp.logical_not(low)).astype(F32).astype(BF16)
    for half in range(2):
        slot_d, slot_u = back_slot(FAR_DOWN, half, 0), back_slot(FAR_UP, half, 0)
        landed(sums.at[0, slot_d], back_recv.at[0, slot_d])
        landed(sums.at[1, slot_u], back_recv.at[1, slot_u])
        total[...] = (
            partial[z, half].astype(F32) + sums[0, slot_d].astype(F32) + sums[1, slot_u].astype(F32)
        ).astype(BF16)
        got = jnp.dot(unfold0, total[:, :hw], preferred_element_type=F32) + jnp.dot(
            unfold1, total[:, hw:], preferred_element_type=F32
        )
        returning[half * (E // 2):(half + 1) * (E // 2)] = got.astype(BF16).reshape(E // 2, 16, hw)

    for i, (yy, xx) in enumerate(peers):
        peer = yy * NX + xx
        send(returning.at[peer], returned.at[e], ret_send.at[i], ret_recv.at[e], peer * NZ + z)
    own_back = pltpu.make_async_copy(returning.at[e], returned.at[e], load_sem.at[5])
    own_back.start()
    plane4(0)
    plane4(1)
    place = place_ref[...]
    token_iota = lax.broadcasted_iota(jnp.int32, (rows, E * 16), 1)
    put0 = (token_iota == place).astype(F32).astype(BF16)
    put1 = (token_iota == place + 8).astype(F32).astype(BF16)
    own_back.wait()
    for yy, xx in peers:
        peer = yy * NX + xx
        landed(returned.at[peer], ret_recv.at[peer])
    gate = gate_ref[...]
    for half, put in enumerate((put0, put1)):
        for j in range(hw // 256):
            c = j * 256
            got = jnp.dot(put, returned[:, :, c:c + 256].reshape(E * 16, 256), preferred_element_type=F32)
            cols = slice(half * hw + c, half * hw + c + 256)
            mixed[:, cols] = hid[:, cols].astype(F32) + got * gate

    def norm_out(i, carry):
        at_rows = pl.ds(pl.multiple_of(i * 32, 32), 32)
        normed[at_rows, :] = norm_rows(mixed[at_rows, :], final_gain[...]).astype(BF16)
        return carry

    lax.fori_loop(0, rows // 32, norm_out, 0)

    def weight_cols(w, cols):
        return weights[w, :, :, :, cols].reshape(width, 256)

    def kv_copy(w):
        return pltpu.make_async_remote_copy(
            src_ref=kv_out.at[w], dst_ref=kv_in.at[w], send_sem=kv_send.at[w], recv_sem=kv_recv.at[w],
            device_id={"grp": 1 - grp}, device_id_type=pl.DeviceIdType.MESH,
        )

    @pl.when(grp == 0)
    def _():
        for w in range(2):
            def project(j, carry):
                cols = pl.ds(pl.multiple_of(j * 256, 256), 256)
                kv_out[w, :, cols] = jnp.dot(
                    normed[...], weight_cols(w, cols), preferred_element_type=F32
                ).astype(BF16)
                return carry

            lax.fori_loop(0, hw // 256, project, 0)
            kv_copy(w).start()
        out_ref[...] = normed[...]
        for w in range(2):
            kv_copy(w).wait_send()

    @pl.when(grp == 1)
    def _():
        def project(j, carry):
            cols = pl.ds(pl.multiple_of(j * 256, 256), 256)
            query[:, cols] = jnp.dot(
                normed[:ROWS_Q, :], weight_cols(0, cols), preferred_element_type=F32
            ).astype(BF16)
            return carry

        lax.fori_loop(0, hw // 256, project, 0)
        out_ref[ROWS_Q:, :] = mixed[ROWS_Q:, :].astype(BF16)

        q_pos = lax.broadcasted_iota(jnp.int32, (ROWS_Q, 1), 0)
        k_pos = lax.broadcasted_iota(jnp.int32, (1, rows), 1)
        seg_q = jnp.zeros((ROWS_Q, 1), jnp.int32)
        seg_k = jnp.zeros((1, rows), jnp.int32)
        q_end = jnp.zeros((1, 1), jnp.int32)
        k_end = jnp.zeros((1, 1), jnp.int32)
        for i in range(SENT):
            q_end = q_end + tgt_ref[:, i:i + 1]
            k_end = k_end + src_ref[:, i:i + 1]
            seg_q = seg_q + jnp.where(q_pos >= q_end, 1, 0)
            seg_k = seg_k + jnp.where(k_pos >= k_end, 1, 0)
        valid = seg_q < SENT
        allowed = (seg_q == seg_k) & valid
        for w in range(2):
            kv_copy(w).wait_recv()
        for h in range(hw // HD):
            cols = slice(h * HD, (h + 1) * HD)
            scores = lax.dot_general(
                query[:, cols], kv_in[0, :, cols], (((1,), (1,)), ((), ())), preferred_element_type=F32
            ) * HD ** (-0.5)
            scores = jnp.where(allowed, scores, -1e30)
            top = jnp.max(scores, axis=-1, keepdims=True)
            expd = jnp.exp(scores - top)
            prob = (expd / jnp.sum(expd, axis=-1, keepdims=True)).astype(BF16)
            context[:, cols] = jnp.dot(prob, kv_in[1, :, cols], preferred_element_type=F32).astype(BF16)
        for j in range(width // 256):
            cols = slice(j * 256, (j + 1) * 256)
            wo_rows = weights[1, j * 2:(j + 1) * 2].reshape(256, hw)
            attended = lax.dot_general(
                context[...], wo_rows, (((1,), (1,)), ((), ())), preferred_element_type=F32
            )
            attended = jnp.where(valid, attended, 0.0)
            out_ref[:ROWS_Q, cols] = (mixed[:ROWS_Q, cols] + attended).astype(BF16)

    for copy in sent:
        copy.wait_send()


def body(
    hidden, norm_gain, final_gain, router, w_in, w_out, expert_ids, slot_ids, src_len, tgt_len, wq, wk, wv, wo,
):
    rows, width = hidden.shape[1:]
    hw = wq.shape[1]
    ff = w_in.shape[2]
    vmem = pl.BlockSpec(memory_space=pltpu.VMEM)
    anywhere = pl.BlockSpec(memory_space=pl.ANY)
    dma = pltpu.SemaphoreType.DMA
    out = pl.pallas_call(
        kernel,
        out_shape=jax.ShapeDtypeStruct((rows, width), BF16),
        in_specs=[anywhere, vmem, vmem, anywhere, anywhere, anywhere] + [vmem] * 8,
        out_specs=vmem,
        scratch_shapes=[
            pltpu.VMEM((rows, width), BF16),
            pltpu.VMEM((rows, width), BF16),
            pltpu.VMEM((width, 128), BF16),
            pltpu.VMEM((width, ff), BF16),
            pltpu.VMEM((ff, width), BF16),
            pltpu.VMEM((E, 16, hw), BF16),
            pltpu.VMEM((E, 16, hw), BF16),
            pltpu.VMEM((NZ, 2, HALF, width), BF16),
            pltpu.VMEM((NZ, 2, HALF, width), BF16),
            pltpu.VMEM((2, 7, HALF, width), BF16),
            pltpu.VMEM((2 * HALF, ff), BF16),
            pltpu.VMEM((HALF, width), BF16),
            pltpu.VMEM((E, 16, hw), BF16),
            pltpu.VMEM((E, 16, hw), BF16),
            pltpu.VMEM((rows, width), F32),
            pltpu.VMEM((2, E, NZ, 16, hw), BF16),
            pltpu.VMEM((2, rows, hw), BF16),
            pltpu.VMEM((2, rows, hw), BF16),
            pltpu.VMEM((ROWS_Q, hw), BF16),
            pltpu.VMEM((ROWS_Q, hw), BF16),
            pltpu.VMEM((rows, 1), F32),
            pltpu.VMEM((rows, 1), jnp.int32),
            dma((6,)),
            dma((15,)),
            dma((E,)),
            dma((2, 7)),
            dma((2, 7)),
            dma((2, 7)),
            dma((2, 7)),
            dma((2, 7)),
            dma((2, 7)),
            dma((48,)),
            dma((2, E, 2)),
            dma((15,)),
            dma((E,)),
            dma((2,)),
            dma((2,)),
        ],
        compiler_params=pltpu.CompilerParams(
            collective_id=0, has_side_effects=True, vmem_limit_bytes=56 * 1024 * 1024
        ),
        cost_estimate=pl.CostEstimate(flops=10**10, bytes_accessed=12 * 10**6, transcendentals=10**6),
    )(
        hidden[0], norm_gain, final_gain, router[0], w_in[0], w_out[0], expert_ids[0].T, slot_ids[0].T,
        src_len, tgt_len, wq, wk, wv, wo,
    )
    return out[None]


def solution(mesh):
    in_specs = (
        P("grp", "ep", None),
        P("grp", None),
        P("grp", None),
        P("grp", None, None),
        P("grp", None, "ep"),
        P("grp", "ep", None),
        P("grp", "ep", None),
        P("grp", "ep", None),
        P("ep", None),
        P("ep", None),
        P("ep", None),
        P("ep", None),
        P("ep", None),
        P("ep", None),
    )
    out_specs = P("grp", "ep", None)
    return jax.shard_map(body, mesh=mesh, in_specs=in_specs, out_specs=out_specs, check_vma=False)
```

time: 532 us -> 110 us (0.21)
  waiting for transfers between devices: 419 us -> 0 us
  Pallas kernels: 0 us -> 108 us
  matrix products: 35.4 us -> 0 us
  starting transfers between devices: 26 us -> 0 us
  local copies, waits for them, and re-layouts: 24.4 us -> 2.3 us
  between operations: 13.4 us -> 0.01 us
  other arithmetic: 10.2 us -> 0 us
    all_to_all x2 -> x0, waiting for transfers between devices: 205 us -> none  [the longest x1 106 us: body(): lax.all_to_all(outgoing, 'ep', split_axis=0, concat_axis=0, tiled=True)]
    all_gather x4 -> x0, waiting for transfers between devices: 204 us -> none  [the longest x1 108 us: body(): lax.all_gather(wo, 'ep', axis=0, tiled=True)]
    pallas_call x0 -> x1, Pallas kernels: none -> 108 us  [body(): pl.pallas_call(kernel, out_shape=jax.ShapeDtypeStruct((rows, width), BF16...]
    dot_general x9 -> x0, matrix products: 32.2 us -> none  [the longest x1 6.69 us: body(): jnp.dot(flat, w_in[0], preferred_element_type=jnp.float32)]
    all_to_all x2 -> x0, starting transfers between devices: 24.4 us -> none  [the longest x1 16.9 us: body(): lax.all_to_all(outgoing, 'ep', split_axis=0, concat_axis=0, tiled=True)]
    reshape x4 -> x0, local copies, waits for them, and re-layouts: 12.9 us -> none  [the longest x1 6.34 us: body(): flat = arrived.reshape(-1, width)]
    reduce_sum x8 -> x0, other arithmetic: 8.22 us -> none  [the longest x2 3.79 us: normalize(): mean = jnp.mean(values, -1, keepdims=True)]
    ppermute x1 -> x0, waiting for transfers between devices: 7.03 us -> none  [shifted(): lax.ppermute(value, axis, [(source, source + steps) for source in range(f...]
  transfers between devices with their start and end apart: 7 -> 0, of which waited for: 5 -> 0; matrix products, arithmetic and copies ran while one was open for 12% -> 0% of each run, Pallas kernels for 0% -> 0%
where the time goes in v1:
time: 110 us
  Pallas kernels  108 us (98%)
  local copies, waits for them, and re-layouts  2.3 us (2%)
    pallas_call x1, Pallas kernels, body(): pl.pallas_call(kernel, out_shape=jax.ShapeDtypeStruct((rows, width), BF16...  108 us
    unnamed x1, local copies, waits for them, and re-layouts  2.3 us

profile of v1, /device:TPU:1, one launch (start us, length us, event | category | flops | bytes accessed | tf_op | source)
XLA Modules:
  0.0 110.2 jit_solution(13440661280773032643)
XLA Ops:
  0.0 107.8 %shard_map.136 = bf16[256,2048]{1,0:T(8,128)(2,1)} custom-call(bf16[256,2048]{1,0:T(8,128)(2,1)} %bitcast.14, f32[1,2048]{1,0:T(1,128)} %norm_gain.1, f32[1,2048]{1,0:T(1,128)} %final_gain.1, bf16[2048,128]{1,0:T(8,128)(2,1)} %bitcast.15, bf16[2048,1024]{1,0:T(8,128)(2,1)} %bitcast.12, bf16[1024,2048]{1,0:T(8,128)(2,1)} %bitcast.13, s32[2,256]{1,0:T(2,128)} %bitcast.16, ...), custom_call_target="tpu_custom_call" | custom-call | flops 10000000000 | bytes 12000000 | tf_op jit(solution)/shard_map/pallas_call | solution.py:472
  107.9 2.3 %copy.16 = bf16[1,256,2048]{2,1,0:T(8,128)(2,1)} copy(bf16[1,256,2048]{2,1,0:T(8,128)(2,1)} %bitcast.11) | data formatting | bytes 2097152

commit v2 on v1

v2 whole, which is shorter than its diff:
```python
import jax
import jax.numpy as jnp
from jax import lax
from jax.experimental import pallas as pl
from jax.experimental.pallas import tpu as pltpu
from jax.sharding import PartitionSpec as P

NY, NX, NZ = 4, 4, 8
E = NY * NX
C = 6
TRIO = C // 2
HALF = E * TRIO
SENT = 4
HD = 128
ROWS_Q = 176
F32 = jnp.float32
BF16 = jnp.bfloat16

RING = [(0, 1), (1, 1), (0, 2), (1, 2), (0, 3), (1, 3), (0, 4), (1, 4)]
BACK = [
    (0, 3, "near"), (1, 3, "near"), (0, 4, "far"), (1, 4, "far"), (0, 3, "far"), (1, 3, "far"),
    (0, 2, "all"), (1, 2, "all"), (0, 1, "all"), (1, 1, "all"),
]


def norm_rows(v, gain):
    mean = jnp.mean(v, -1, keepdims=True)
    centred = v - mean
    spread = jnp.mean(centred * centred, -1, keepdims=True)
    return centred * lax.rsqrt(spread + 1e-05) * gain


def one_hot(hit):
    return hit.astype(F32).astype(BF16)


def kernel(
    hidden_hbm, norm_gain, final_gain, router_hbm, w_in_hbm, w_out_hbm, ids_ref, slots_ref, src_ref, tgt_ref,
    wq_hbm, wk_hbm, wv_hbm, wo_hbm,
    out_ref,
    hid, normed, router, w_in, w_out, packed, arrived, tokens, partial, sums, inner, total, returning, returned,
    mixed, weights, kv_out, kv_in, query, context, gate_ref, pick, put, fold, unfold,
    load_sem, pack_send, pack_recv, ring_send, ring_recv, back_send, back_recv, wz_send, wz_recv,
    wxy_send, wxy_recv, ret_send, ret_recv, kv_send, kv_recv,
):
    rows, width = hid.shape
    hw = width // 2
    quarter = width // 4
    ep = lax.axis_index("ep")
    grp = lax.axis_index("grp")
    z = lax.rem(ep, NZ)
    e = ep // NZ
    x = lax.rem(e, NX)
    y = e // NX

    def at(yy, xx, zz):
        return (yy * NX + xx) * NZ + zz

    def zmod(v):
        return lax.rem(v + NZ, NZ)

    def xmod(v):
        return lax.rem(v + NX, NX)

    def remote(src, dst, send, recv, target):
        return pltpu.make_async_remote_copy(
            src_ref=src, dst_ref=dst, send_sem=send, recv_sem=recv,
            device_id={"ep": target}, device_id_type=pl.DeviceIdType.MESH,
        )

    sent = []

    def send(*args):
        copy = remote(*args)
        copy.start()
        sent.append(copy)

    def landed(dst, recv):
        remote(dst, dst, kv_send.at[0], recv, ep).wait_recv()

    z_up, z_down = at(y, x, zmod(z + 1)), at(y, x, zmod(z - 1))
    peers = []
    for dy in (2, 1, 3, 0):
        for dx in (2, 1, 3, 0):
            if dy or dx:
                peers.append((xmod(y + dy), xmod(x + dx)))

    load_hidden = pltpu.make_async_copy(hidden_hbm, hid, load_sem.at[0])
    load_router = pltpu.make_async_copy(router_hbm, router, load_sem.at[1])
    load_in = pltpu.make_async_copy(w_in_hbm, w_in, load_sem.at[2])
    load_out = pltpu.make_async_copy(w_out_hbm, w_out, load_sem.at[3])

    def load_rows(w, source):
        return pltpu.make_async_copy(source, weights.at[w, e, z], load_sem.at[4 + w])

    load_hidden.start()

    @pl.when(grp == 0)
    def _():
        load_rows(0, wk_hbm).start()
        load_rows(1, wv_hbm).start()

    @pl.when(grp == 1)
    def _():
        load_rows(0, wq_hbm).start()
        load_rows(1, wo_hbm).start()

    barrier = pltpu.get_barrier_semaphore()
    for target in [at(yy, xx, z) for yy, xx in peers] + [at(y, x, zmod(z + k)) for k in (-2, -1, 1, 2)]:
        pl.semaphore_signal(barrier, inc=1, device_id={"ep": target}, device_id_type=pl.DeviceIdType.MESH)
    pl.semaphore_signal(barrier, inc=1, device_id={"grp": 1 - grp}, device_id_type=pl.DeviceIdType.MESH)
    load_router.start()
    load_in.start()
    load_out.start()

    ids_row = ids_ref[...]
    slots_row = slots_ref[...]
    spots = []
    for half in range(2):
        live_row = (slots_row >= half * TRIO) & (slots_row < (half + 1) * TRIO)
        spot = jnp.where(live_row, ids_row * 16 + slots_row - half * TRIO, -1000)
        spots.append(jnp.max(spot, axis=0, keepdims=True))
    stacked = jnp.concatenate([ids_row, slots_row] + spots + spots, axis=0)
    columns = jnp.transpose(stacked.astype(F32)).astype(jnp.int32)
    ids, live = columns[:, 0:2], columns[:, 2:4] >= 0
    slot_iota = lax.broadcasted_iota(jnp.int32, (E * 16, rows), 0)
    for half in range(2):
        for q in range(4):
            pick[half, q] = one_hot(slot_iota == spots[half] + 4 * q)
    r_iota = lax.broadcasted_iota(jnp.int32, (HALF, E * 16), 0)
    q_iota = lax.broadcasted_iota(jnp.int32, (HALF, E * 16), 1)
    base = (r_iota // TRIO) * 16 + r_iota % TRIO
    for q in range(4):
        fold[q] = one_hot(q_iota == base + 4 * q)

    pl.semaphore_wait(barrier, len(peers) + 5)
    load_rows(0, wq_hbm).wait()
    load_rows(1, wq_hbm).wait()

    def ways():
        return enumerate(((1, z_up), (-1, z_down)))

    def part(ref, way, k):
        if k < 4:
            return ref
        size = ref.shape[-1] // 2
        return ref.at[:, pl.ds(way * size, size)]

    def wz_send_rows(w, block, way, reach, dist):
        ref = part(weights.at[w, e, block], way, dist)
        target = at(y, x, zmod(z + (reach, -reach)[way]))
        send(ref, ref, wz_send.at[w, way, dist - 1], wz_recv.at[w, way, dist - 1], target)

    def wz_wait(w, way, dist):
        block = zmod(z - (dist, -dist)[way])
        landed(part(weights.at[w, e, block], way, dist), wz_recv.at[w, way, dist - 1])

    def wz_near():
        for dist in (2, 1):
            for w in range(2):
                for way in range(2):
                    wz_send_rows(w, z, way, dist, dist)

    def wz_far():
        for w in range(2):
            for way in range(2):
                wz_wait(w, way, 2)
                block = zmod(z - (2, -2)[way])
                wz_send_rows(w, block, way, 1, 3)
                wz_send_rows(w, block, way, 2, 4)

    def wz_end():
        for w in range(2):
            for way in range(2):
                for dist in (1, 3, 4):
                    wz_wait(w, way, dist)

    wz_near()

    load_hidden.wait()

    def norm_in(i, carry):
        at_rows = pl.ds(pl.multiple_of(i * 32, 32), 32)
        normed[at_rows, :] = norm_rows(hid[at_rows, :].astype(F32), norm_gain[...]).astype(BF16)
        return carry

    lax.fori_loop(0, rows // 32, norm_in, 0)

    own_slots = [pltpu.make_async_copy(packed.at[h, e], arrived.at[h, e], load_sem.at[6 + h]) for h in range(2)]
    own_back = [
        pltpu.make_async_copy(returning.at[h, e], returned.at[h, e], load_sem.at[8 + h]) for h in range(2)
    ]
    for half in range(2):
        for j in range(quarter // 256):
            got = jnp.zeros((E * 16, 256), F32)
            for q in range(4):
                c = q * quarter + j * 256
                got = got + jnp.dot(pick[half, q], normed[:, c:c + 256], preferred_element_type=F32)
            packed[half, :, :, j * 256:(j + 1) * 256] = got.astype(BF16).reshape(E, 16, 256)
        for i, (yy, xx) in enumerate(peers):
            peer = yy * NX + xx
            send(
                packed.at[half, peer], arrived.at[half, e], pack_send.at[half, i], pack_recv.at[half, e],
                peer * NZ + z,
            )
        own_slots[half].start()

    def slots_in(half):
        own_slots[half].wait()
        for yy, xx in peers:
            peer = yy * NX + xx
            landed(arrived.at[half, peer], pack_recv.at[half, peer])
        got = arrived[half].reshape(E * 16, quarter)
        for q in range(4):
            tokens[z, half, :, q * quarter:(q + 1) * quarter] = jnp.dot(
                fold[q], got, preferred_element_type=F32
            ).astype(BF16)

    def ring_hop(slot):
        half, k = RING[slot]
        for way, (sign, target) in ways():
            ref = part(tokens.at[zmod(z - sign * (k - 1)), half], way, k)
            send(ref, ref, ring_send.at[way, slot], ring_recv.at[way, slot], target)

    def ring_wait(slot):
        half, k = RING[slot]
        for way, (sign, _) in ways():
            landed(part(tokens.at[zmod(z - sign * k), half], way, k), ring_recv.at[way, slot])

    def expert(parts):
        count = len(parts) * HALF

        def first_step(j, carry):
            cols = pl.ds(pl.multiple_of(j * 256, 256), 256)
            blocks = [tokens[block, half] for block, half in parts]
            both = jnp.concatenate(blocks, axis=0) if len(blocks) > 1 else blocks[0]
            got = jnp.dot(both, w_in[:, cols], preferred_element_type=F32)
            inner[:count, cols] = jnp.maximum(got, 0.0).astype(BF16)
            return carry

        def second_step(j, carry):
            cols = pl.ds(pl.multiple_of(j * 256, 256), 256)
            got = jnp.dot(inner[:count, :], w_out[:, cols], preferred_element_type=F32).astype(BF16)
            for i, (block, half) in enumerate(parts):
                partial[block, half, :, cols] = got[i * HALF:(i + 1) * HALF]
            return carry

        lax.fori_loop(0, w_in.shape[1] // 256, first_step, 0)
        lax.fori_loop(0, width // 256, second_step, 0)

    def expert_slot(slot):
        half, k = RING[slot]
        expert([(zmod(z - k), half), (zmod(z + k), half)] if k < 4 else [(zmod(z + k), half)])

    def block_at(w, a, b):
        xx, yy = (xmod(x + a), xmod(y + b)) if w == 0 else (xmod(x + b), xmod(y + a))
        return yy * NX + xx

    def go(w, phase, sign):
        if (w == 0) == (phase == 0):
            return at(y, xmod(x + sign), z)
        return at(xmod(y + sign), x, z)

    w_count = [0]

    def wxy(w, a, b, piece, phase, sign):
        blk = block_at(w, a, b)
        ref = weights.at[w, blk] if piece is None else weights.at[w, blk, pl.ds(piece * 4, 4)]
        send(ref, ref, wxy_send.at[w_count[0]], wxy_recv.at[w, blk, piece or 0], go(w, phase, sign))
        w_count[0] += 1

    def wxy_wait(w, a, b):
        blk = block_at(w, a, b)
        opposite = b == 2 or (b == 0 and a == 2)
        if opposite:
            for piece in range(2):
                landed(weights.at[w, blk, pl.ds(piece * 4, 4)], wxy_recv.at[w, blk, piece])
        else:
            landed(weights.at[w, blk], wxy_recv.at[w, blk, 0])

    def forward(w, a, b, phase):
        if phase == 0:
            wxy(w, a, b, 0 if a == 1 else 1, 0, -1 if a == 1 else 1)
        else:
            wxy(w, a, b, 0 if b == 1 else 1, 1, -1 if b == 1 else 1)

    def plane0():
        for w in range(2):
            for phase in range(2):
                for sign in (1, -1):
                    wxy(w, 0, 0, None, phase, sign)

    def plane1():
        for w in range(2):
            for a in (1, 3):
                wxy_wait(w, a, 0)
                forward(w, a, 0, 0)
        for w in range(2):
            for b in (1, 3):
                wxy_wait(w, 0, b)
                forward(w, 0, b, 1)
        for w in range(2):
            for a in (1, 3):
                for sign in (1, -1):
                    wxy(w, a, 0, None, 1, sign)

    def plane2():
        for w in range(2):
            wxy_wait(w, 2, 0)
            for sign in (1, -1):
                wxy(w, 2, 0, None, 1, sign)
        for w in range(2):
            for a in (1, 3):
                for b in (1, 3):
                    wxy_wait(w, a, b)
                    forward(w, a, b, 1)

    def plane3():
        for w in range(2):
            for b in (1, 3):
                wxy_wait(w, 2, b)
                forward(w, 2, b, 1)

    def plane4(w):
        for a in range(4):
            wxy_wait(w, a, 2)

    wz_far()
    def columns_of(ref, way, kind):
        if kind == "all":
            return ref
        size = ref.shape[-1] // 2
        return ref.at[:, pl.ds((way if kind == "far" else 1 - way) * size, size)]

    def back_step(step):
        half, k, kind = BACK[step]
        for way, (sign, target) in enumerate(((1, z_down), (-1, z_up))):
            here = columns_of(partial.at[zmod(z - sign * k), half], way, kind)
            came = columns_of(sums.at[way, half, min(k, 3)], way, kind)
            if k == 2:
                for i, other in enumerate(("far", "near")):
                    landed(columns_of(sums.at[way, half, 2], way, other), back_recv.at[way, half, 2, i])
            elif k == 1 or (k == 3 and kind == "far"):
                landed(came, back_recv.at[way, half, k, 0])
            if k < 3 or (k == 3 and kind == "far"):
                here[...] = (here[...].astype(F32) + came[...].astype(F32)).astype(BF16)
            send(
                here, columns_of(sums.at[way, half, k - 1], way, kind), back_send.at[way, step],
                back_recv.at[way, half, k - 1, 1 if kind == "near" else 0], target,
            )

    slots_in(0)
    ring_hop(0)
    slots_in(1)
    ring_hop(1)
    load_in.wait()
    load_out.wait()
    wz_end()
    plane0()
    expert([(z, 0), (z, 1)])
    for slot in range(6):
        ring_wait(slot)
        ring_hop(slot + 2)
        if slot == 5:
            back_step(0)
        expert_slot(slot)
        if slot == 0:
            load_router.wait()
            logits = jnp.dot(normed[...], router[...], preferred_element_type=F32)
            lane = lax.broadcasted_iota(jnp.int32, logits.shape, 1)
            pick_a = jnp.sum(jnp.where(lane == ids[:, 0:1], logits, 0.0), axis=1, keepdims=True)
            pick_b = jnp.sum(jnp.where(lane == ids[:, 1:2], logits, 0.0), axis=1, keepdims=True)
            gate_ref[...] = jnp.where(live[:, 0:1], jax.nn.sigmoid(pick_a - pick_b), 0.0) + jnp.where(
                live[:, 1:2], jax.nn.sigmoid(pick_b - pick_a), 0.0
            )
        if slot == 1:
            token_iota = lax.broadcasted_iota(jnp.int32, (rows, E * 16), 1)
            for half in range(2):
                for q in range(4):
                    put[half, q] = one_hot(token_iota == columns[:, 4 + half:5 + half] + 4 * q)
        if slot == 2:
            b_iota = lax.broadcasted_iota(jnp.int32, (E * 16, HALF), 0)
            s_iota = lax.broadcasted_iota(jnp.int32, (E * 16, HALF), 1)
            origin = (s_iota // TRIO) * 16 + s_iota % TRIO
            for q in range(4):
                unfold[q] = one_hot(b_iota == origin + 4 * q)
        if slot == 3:
            plane1()

    back_step(1)
    ring_wait(6)
    ring_wait(7)
    expert([(zmod(z + 4), 0), (zmod(z + 4), 1)])
    back_step(2)
    back_step(3)
    plane2()
    for step in range(4, len(BACK)):
        back_step(step)
        if step == 6:
            plane3()

    for half in range(2):
        for way in range(2):
            landed(sums.at[way, half, 0], back_recv.at[way, half, 0, 0])
        total[...] = (
            partial[z, half].astype(F32) + sums[0, half, 0].astype(F32) + sums[1, half, 0].astype(F32)
        ).astype(BF16)
        got = jnp.zeros((E * 16, quarter), F32)
        for q in range(4):
            got = got + jnp.dot(
                unfold[q], total[:, q * quarter:(q + 1) * quarter], preferred_element_type=F32
            )
        returning[half] = got.astype(BF16).reshape(E, 16, quarter)
        for i, (yy, xx) in enumerate(peers):
            peer = yy * NX + xx
            send(
                returning.at[half, peer], returned.at[half, e], ret_send.at[half, i], ret_recv.at[half, e],
                peer * NZ + z,
            )
        own_back[half].start()
    plane4(0)
    for half in range(2):
        own_back[half].wait()
        for yy, xx in peers:
            peer = yy * NX + xx
            landed(returned.at[half, peer], ret_recv.at[half, peer])
        gate = gate_ref[...]
        for q in range(4):
            for j in range(quarter // 256):
                got = jnp.dot(
                    put[half, q], returned[half, :, :, j * 256:(j + 1) * 256].reshape(E * 16, 256),
                    preferred_element_type=F32,
                )
                c = q * quarter + j * 256
                before = mixed[:, c:c + 256] if half else hid[:, c:c + 256].astype(F32)
                mixed[:, c:c + 256] = before + got * gate

    def norm_out(i, carry):
        at_rows = pl.ds(pl.multiple_of(i * 32, 32), 32)
        normed[at_rows, :] = norm_rows(mixed[at_rows, :], final_gain[...]).astype(BF16)
        return carry

    lax.fori_loop(0, rows // 32, norm_out, 0)
    plane4(1)

    groups = hw // 256

    def weight_cols(w, j):
        return weights[w, :, :, :, j * 256:(j + 1) * 256].reshape(width, 256)

    def kv_copy(j):
        return pltpu.make_async_remote_copy(
            src_ref=kv_out.at[j], dst_ref=kv_in.at[j], send_sem=kv_send.at[j], recv_sem=kv_recv.at[j],
            device_id={"grp": 1 - grp}, device_id_type=pl.DeviceIdType.MESH,
        )

    @pl.when(grp == 0)
    def _():
        for j in range(groups):
            for w in range(2):
                kv_out[j, w] = jnp.dot(
                    normed[...], weight_cols(w, j), preferred_element_type=F32
                ).astype(BF16)
            kv_copy(j).start()
        out_ref[...] = normed[...]
        for j in range(groups):
            kv_copy(j).wait_send()

    @pl.when(grp == 1)
    def _():
        for j in range(groups):
            query[j] = jnp.dot(
                normed[:ROWS_Q, :], weight_cols(0, j), preferred_element_type=F32
            ).astype(BF16)
        out_ref[ROWS_Q:, :] = mixed[ROWS_Q:, :].astype(BF16)

        q_pos = lax.broadcasted_iota(jnp.int32, (ROWS_Q, 1), 0)
        k_pos = lax.broadcasted_iota(jnp.int32, (1, rows), 1)
        seg_q = jnp.zeros((ROWS_Q, 1), jnp.int32)
        seg_k = jnp.zeros((1, rows), jnp.int32)
        q_end = jnp.zeros((1, 1), jnp.int32)
        k_end = jnp.zeros((1, 1), jnp.int32)
        for i in range(SENT):
            q_end = q_end + tgt_ref[:, i:i + 1]
            k_end = k_end + src_ref[:, i:i + 1]
            seg_q = seg_q + jnp.where(q_pos >= q_end, 1, 0)
            seg_k = seg_k + jnp.where(k_pos >= k_end, 1, 0)
        valid = seg_q < SENT
        allowed = (seg_q == seg_k) & valid
        for h in range(hw // HD):
            j, cols = h // 2, slice(h % 2 * HD, (h % 2 + 1) * HD)
            if h % 2 == 0:
                kv_copy(j).wait_recv()
            scores = lax.dot_general(
                query[j, :, cols], kv_in[j, 0, :, cols], (((1,), (1,)), ((), ())), preferred_element_type=F32
            ) * HD ** (-0.5)
            scores = jnp.where(allowed, scores, -1e30)
            top = jnp.max(scores, axis=-1, keepdims=True)
            expd = jnp.exp(scores - top)
            prob = (expd / jnp.sum(expd, axis=-1, keepdims=True)).astype(BF16)
            context[:, h * HD:(h + 1) * HD] = jnp.dot(
                prob, kv_in[j, 1, :, cols], preferred_element_type=F32
            ).astype(BF16)
        for j in range(width // 256):
            cols = slice(j * 256, (j + 1) * 256)
            wo_rows = weights[1, j * 2:(j + 1) * 2].reshape(256, hw)
            attended = lax.dot_general(
                context[...], wo_rows, (((1,), (1,)), ((), ())), preferred_element_type=F32
            )
            attended = jnp.where(valid, attended, 0.0)
            out_ref[:ROWS_Q, cols] = (mixed[:ROWS_Q, cols] + attended).astype(BF16)

    for copy in sent:
        copy.wait_send()


def body(
    hidden, norm_gain, final_gain, router, w_in, w_out, expert_ids, slot_ids, src_len, tgt_len, wq, wk, wv, wo,
):
    rows, width = hidden.shape[1:]
    hw = wq.shape[1]
    ff = w_in.shape[2]
    vmem = pl.BlockSpec(memory_space=pltpu.VMEM)
    anywhere = pl.BlockSpec(memory_space=pl.ANY)
    dma = pltpu.SemaphoreType.DMA
    out = pl.pallas_call(
        kernel,
        out_shape=pltpu.VMEM((rows, width), BF16),
        in_specs=[anywhere, vmem, vmem, anywhere, anywhere, anywhere] + [vmem] * 4 + [anywhere] * 4,
        out_specs=vmem,
        scratch_shapes=[
            pltpu.VMEM((rows, width), BF16),
            pltpu.VMEM((rows, width), BF16),
            pltpu.VMEM((width, 128), BF16),
            pltpu.VMEM((width, ff), BF16),
            pltpu.VMEM((ff, width), BF16),
            pltpu.VMEM((2, E, 16, width // 4), BF16),
            pltpu.VMEM((2, E, 16, width // 4), BF16),
            pltpu.VMEM((NZ, 2, HALF, width), BF16),
            pltpu.VMEM((NZ, 2, HALF, width), BF16),
            pltpu.VMEM((2, 2, 4, HALF, width), BF16),
            pltpu.VMEM((2 * HALF, ff), BF16),
            pltpu.VMEM((HALF, width), BF16),
            pltpu.VMEM((2, E, 16, width // 4), BF16),
            pltpu.VMEM((2, E, 16, width // 4), BF16),
            pltpu.VMEM((rows, width), F32),
            pltpu.VMEM((2, E, NZ, 16, hw), BF16),
            pltpu.VMEM((hw // 256, 2, rows, 256), BF16),
            pltpu.VMEM((hw // 256, 2, rows, 256), BF16),
            pltpu.VMEM((hw // 256, ROWS_Q, 256), BF16),
            pltpu.VMEM((ROWS_Q, hw), BF16),
            pltpu.VMEM((rows, 1), F32),
            pltpu.VMEM((2, 4, E * 16, rows), BF16),
            pltpu.VMEM((2, 4, rows, E * 16), BF16),
            pltpu.VMEM((4, HALF, E * 16), BF16),
            pltpu.VMEM((4, E * 16, HALF), BF16),
            dma((10,)),
            dma((2, 15)),
            dma((2, E)),
            dma((2, 8)),
            dma((2, 8)),
            dma((2, len(BACK))),
            dma((2, 2, 4, 2)),
            dma((2, 2, 4)),
            dma((2, 2, 4)),
            dma((40,)),
            dma((2, E, 2)),
            dma((2, 15)),
            dma((2, E)),
            dma((hw // 256,)),
            dma((hw // 256,)),
        ],
        compiler_params=pltpu.CompilerParams(
            collective_id=0, has_side_effects=True, vmem_limit_bytes=56 * 1024 * 1024
        ),
        cost_estimate=pl.CostEstimate(flops=10**10, bytes_accessed=12 * 10**6, transcendentals=10**6),
    )(
        hidden[0], norm_gain, final_gain, router[0], w_in[0], w_out[0], expert_ids[0].T, slot_ids[0].T,
        src_len, tgt_len, wq, wk, wv, wo,
    )
    return out[None]


def solution(mesh):
    in_specs = (
        P("grp", "ep", None),
        P("grp", None),
        P("grp", None),
        P("grp", None, None),
        P("grp", None, "ep"),
        P("grp", "ep", None),
        P("grp", "ep", None),
        P("grp", "ep", None),
        P("ep", None),
        P("ep", None),
        P("ep", None),
        P("ep", None),
        P("ep", None),
        P("ep", None),
    )
    out_specs = P("grp", "ep", None)
    return jax.shard_map(body, mesh=mesh, in_specs=in_specs, out_specs=out_specs, check_vma=False)
```

time: 110 us -> 101 us (0.918)
  Pallas kernels: 108 us -> 99.9 us
  local copies, waits for them, and re-layouts: 2.3 us -> 0.97 us
    pallas_call x1, Pallas kernels: 108 us -> 99.9 us  [body(): pl.pallas_call(kernel, out_shape=pltpu.VMEM((rows, width), BF16), in_spec...]
    unnamed x1, local copies, waits for them, and re-layouts: 2.3 us -> 0.97 us
where the time goes in v2:
time: 101 us
  Pallas kernels  99.9 us (99%)
    pallas_call x1, Pallas kernels, body(): pl.pallas_call(kernel, out_shape=pltpu.VMEM((rows, width), BF16), in_spec...  99.9 us

profile of v2, /device:TPU:1, one launch (start us, length us, event | category | flops | bytes accessed | tf_op | source)
XLA Modules:
  0.0 100.9 jit_solution(17675304233969751465)
XLA Ops:
  0.0 99.9 %shard_map.136 = bf16[256,2048]{1,0:T(8,128)(2,1)S(1)} custom-call(bf16[256,2048]{1,0:T(8,128)(2,1)} %bitcast.14, f32[1,2048]{1,0:T(1,128)} %norm_gain.1, f32[1,2048]{1,0:T(1,128)} %final_gain.1, bf16[2048,128]{1,0:T(8,128)(2,1)} %bitcast.15, bf16[2048,1024]{1,0:T(8,128)(2,1)} %bitcast.12, bf16[1024,2048]{1,0:T(8,128)(2,1)} %bitcast.13, s32[2,256]{1,0:T(2,128)} %bitcast.16, ...), custom_call_target="tpu_custom_call" | custom-call | flops 10000000000 | bytes 12000000 | tf_op jit(solution)/shard_map/pallas_call | solution.py:526
  99.9 1.0 copy.16

commit v3 on v2

--- a/solution.py
+++ b/solution.py
@@ -8,8 +8,10 @@
 NY, NX, NZ = 4, 4, 8
 E = NY * NX
 C = 6
-TRIO = C // 2
-HALF = E * TRIO
+PAIR = 2 * E
+START = (0, PAIR)
+SIZE = (PAIR, 2 * PAIR)
+PAIRS = ((0,), (1, 2))
 SENT = 4
 HD = 128
 ROWS_Q = 176
@@ -18,8 +20,8 @@
 
 RING = [(0, 1), (1, 1), (0, 2), (1, 2), (0, 3), (1, 3), (0, 4), (1, 4)]
 BACK = [
-    (0, 3, "near"), (1, 3, "near"), (0, 4, "far"), (1, 4, "far"), (0, 3, "far"), (1, 3, "far"),
-    (0, 2, "all"), (1, 2, "all"), (0, 1, "all"), (1, 1, "all"),
+    (0, 3, "near"), (1, 3, "near"), (1, 4, "far"), (0, 4, "far"), (1, 3, "far"), (0, 3, "far"),
+    (1, 2, "all"), (0, 2, "all"), (1, 1, "all"), (0, 1, "all"),
 ]
 
 
@@ -38,14 +40,14 @@
     hidden_hbm, norm_gain, final_gain, router_hbm, w_in_hbm, w_out_hbm, ids_ref, slots_ref, src_ref, tgt_ref,
     wq_hbm, wk_hbm, wv_hbm, wo_hbm,
     out_ref,
-    hid, normed, router, w_in, w_out, packed, arrived, tokens, partial, sums, inner, total, returning, returned,
-    mixed, weights, kv_out, kv_in, query, context, gate_ref, pick, put, fold, unfold,
+    hid, normed, router, w_in, w_out, packed, arrived, tokens, partial, sums, inner, returning, returned,
+    mixed, weights, kv_out, kv_in, query, context, gate_ref, spot_ref, pick, perm, perm_t, back_rows,
     load_sem, pack_send, pack_recv, ring_send, ring_recv, back_send, back_recv, wz_send, wz_recv,
     wxy_send, wxy_recv, ret_send, ret_recv, kv_send, kv_recv,
 ):
     rows, width = hid.shape
     hw = width // 2
-    quarter = width // 4
+    eighth = width // 8
     ep = lax.axis_index("ep")
     grp = lax.axis_index("grp")
     z = lax.rem(ep, NZ)
@@ -115,23 +117,17 @@
 
     ids_row = ids_ref[...]
     slots_row = slots_ref[...]
-    spots = []
-    for half in range(2):
-        live_row = (slots_row >= half * TRIO) & (slots_row < (half + 1) * TRIO)
-        spot = jnp.where(live_row, ids_row * 16 + slots_row - half * TRIO, -1000)
-        spots.append(jnp.max(spot, axis=0, keepdims=True))
-    stacked = jnp.concatenate([ids_row, slots_row] + spots + spots, axis=0)
+    pair_row = jnp.where(slots_row >= 2, 1, 0) + jnp.where(slots_row >= 4, 1, 0)
+    spot = jnp.where(slots_row >= 0, pair_row * (PAIR - 2) + 2 * ids_row + slots_row, -1000)
+    spot = jnp.max(spot, axis=0, keepdims=True)
+    stacked = jnp.concatenate([ids_row, slots_row] + [spot] * 4, axis=0)
     columns = jnp.transpose(stacked.astype(F32)).astype(jnp.int32)
-    ids, live = columns[:, 0:2], columns[:, 2:4] >= 0
-    slot_iota = lax.broadcasted_iota(jnp.int32, (E * 16, rows), 0)
-    for half in range(2):
-        for q in range(4):
-            pick[half, q] = one_hot(slot_iota == spots[half] + 4 * q)
-    r_iota = lax.broadcasted_iota(jnp.int32, (HALF, E * 16), 0)
-    q_iota = lax.broadcasted_iota(jnp.int32, (HALF, E * 16), 1)
-    base = (r_iota // TRIO) * 16 + r_iota % TRIO
-    for q in range(4):
-        fold[q] = one_hot(q_iota == base + 4 * q)
+    ids, live, spot_ref[...] = columns[:, 0:2], columns[:, 2:4] >= 0, columns[:, 4:5]
+    pick[...] = one_hot(lax.broadcasted_iota(jnp.int32, (E * C, rows), 0) == spot)
+    i_iota = lax.broadcasted_iota(jnp.int32, (E * 16, E * 16), 0)
+    j_iota = lax.broadcasted_iota(jnp.int32, (E * 16, E * 16), 1)
+    perm[...] = one_hot(j_iota == (i_iota % 16) // 2 * PAIR + i_iota // 16 * 2 + i_iota % 2)
+    perm_t[...] = one_hot(i_iota == (j_iota % 16) // 2 * PAIR + j_iota // 16 * 2 + j_iota % 2)
 
     pl.semaphore_wait(barrier, len(peers) + 5)
     load_rows(0, wq_hbm).wait()
@@ -180,60 +176,84 @@
     load_hidden.wait()
 
     def norm_in(i, carry):
-        at_rows = pl.ds(pl.multiple_of(i * 32, 32), 32)
-        normed[at_rows, :] = norm_rows(hid[at_rows, :].astype(F32), norm_gain[...]).astype(BF16)
+        for j in range(4):
+            at_rows = pl.ds(pl.multiple_of(i * 64 + j * 16, 16), 16)
+            normed[at_rows, :] = norm_rows(hid[at_rows, :].astype(F32), norm_gain[...]).astype(BF16)
         return carry
 
-    lax.fori_loop(0, rows // 32, norm_in, 0)
-
-    own_slots = [pltpu.make_async_copy(packed.at[h, e], arrived.at[h, e], load_sem.at[6 + h]) for h in range(2)]
-    own_back = [
-        pltpu.make_async_copy(returning.at[h, e], returned.at[h, e], load_sem.at[8 + h]) for h in range(2)
-    ]
-    for half in range(2):
-        for j in range(quarter // 256):
-            got = jnp.zeros((E * 16, 256), F32)
-            for q in range(4):
-                c = q * quarter + j * 256
-                got = got + jnp.dot(pick[half, q], normed[:, c:c + 256], preferred_element_type=F32)
-            packed[half, :, :, j * 256:(j + 1) * 256] = got.astype(BF16).reshape(E, 16, 256)
+    def spread(pair_rows):
+        tall = jnp.concatenate([pair_rows[:, q * eighth:(q + 1) * eighth] for q in range(8)], axis=0)
+        return jnp.dot(perm[...], tall, preferred_element_type=F32).astype(BF16).reshape(E, 16, eighth)
+
+    def gathered(ref, pair):
+        tall = jnp.dot(
+            perm_t[...], ref[:, :, pair * eighth:(pair + 1) * eighth].reshape(E * 16, eighth),
+            preferred_element_type=F32,
+        )
+        return jnp.concatenate([tall[q * PAIR:(q + 1) * PAIR] for q in range(8)], axis=1)
+
+    def piece(ref, block, half):
+        return ref.at[block, pl.ds(START[half], SIZE[half])]
+
+    def exchange(source, target, send_sem, recv_sem, half):
         for i, (yy, xx) in enumerate(peers):
             peer = yy * NX + xx
             send(
-                packed.at[half, peer], arrived.at[half, e], pack_send.at[half, i], pack_recv.at[half, e],
-                peer * NZ + z,
+                pair_cols_at(source, peer, half), pair_cols_at(target, e, half), send_sem.at[half, i],
+                recv_sem.at[half, e], peer * NZ + z,
             )
+
+    def pair_cols_at(ref, block, half):
+        return ref.at[block, :, pl.ds(PAIRS[half][0] * eighth, len(PAIRS[half]) * eighth)]
+
+    def exchanged(target, recv_sem, half):
+        for yy, xx in peers:
+            peer = yy * NX + xx
+            landed(pair_cols_at(target, peer, half), recv_sem.at[half, peer])
+
+    own_slots = [
+        pltpu.make_async_copy(pair_cols_at(packed, e, h), pair_cols_at(arrived, e, h), load_sem.at[6 + h])
+        for h in range(2)
+    ]
+    own_back = [
+        pltpu.make_async_copy(pair_cols_at(returning, e, h), pair_cols_at(returned, e, h), load_sem.at[8 + h])
+        for h in range(2)
+    ]
+    for half in range(2):
+        picked = jnp.dot(
+            pick[START[half]:START[half] + SIZE[half], :], hid[...], preferred_element_type=F32
+        ).astype(BF16)
+        for i, pair in enumerate(PAIRS[half]):
+            packed[:, :, pair * eighth:(pair + 1) * eighth] = spread(picked[i * PAIR:(i + 1) * PAIR])
+        exchange(packed, arrived, pack_send, pack_recv, half)
         own_slots[half].start()
 
     def slots_in(half):
         own_slots[half].wait()
-        for yy, xx in peers:
-            peer = yy * NX + xx
-            landed(arrived.at[half, peer], pack_recv.at[half, peer])
-        got = arrived[half].reshape(E * 16, quarter)
-        for q in range(4):
-            tokens[z, half, :, q * quarter:(q + 1) * quarter] = jnp.dot(
-                fold[q], got, preferred_element_type=F32
+        exchanged(arrived, pack_recv, half)
+        for pair in PAIRS[half]:
+            tokens[z, pair * PAIR:(pair + 1) * PAIR, :] = norm_rows(
+                gathered(arrived, pair), norm_gain[...]
             ).astype(BF16)
 
     def ring_hop(slot):
         half, k = RING[slot]
         for way, (sign, target) in ways():
-            ref = part(tokens.at[zmod(z - sign * (k - 1)), half], way, k)
+            ref = part(piece(tokens, zmod(z - sign * (k - 1)), half), way, k)
             send(ref, ref, ring_send.at[way, slot], ring_recv.at[way, slot], target)
 
     def ring_wait(slot):
         half, k = RING[slot]
         for way, (sign, _) in ways():
-            landed(part(tokens.at[zmod(z - sign * k), half], way, k), ring_recv.at[way, slot])
+            landed(part(piece(tokens, zmod(z - sign * k), half), way, k), ring_recv.at[way, slot])
 
     def expert(parts):
-        count = len(parts) * HALF
+        count = sum(SIZE[half] for _, half in parts)
 
         def first_step(j, carry):
             cols = pl.ds(pl.multiple_of(j * 256, 256), 256)
-            blocks = [tokens[block, half] for block, half in parts]
-            both = jnp.concatenate(blocks, axis=0) if len(blocks) > 1 else blocks[0]
+            blocks = [tokens[block, START[half]:START[half] + SIZE[half]] for block, half in parts]
+            both = jnp.concatenate(blocks, axis=0)
             got = jnp.dot(both, w_in[:, cols], preferred_element_type=F32)
             inner[:count, cols] = jnp.maximum(got, 0.0).astype(BF16)
             return carry
@@ -241,8 +261,10 @@
         def second_step(j, carry):
             cols = pl.ds(pl.multiple_of(j * 256, 256), 256)
             got = jnp.dot(inner[:count, :], w_out[:, cols], preferred_element_type=F32).astype(BF16)
-            for i, (block, half) in enumerate(parts):
-                partial[block, half, :, cols] = got[i * HALF:(i + 1) * HALF]
+            row = 0
+            for block, half in parts:
+                partial[block, START[half]:START[half] + SIZE[half], cols] = got[row:row + SIZE[half]]
+                row += SIZE[half]
             return carry
 
         lax.fori_loop(0, w_in.shape[1] // 256, first_step, 0)
@@ -335,17 +357,17 @@
     def back_step(step):
         half, k, kind = BACK[step]
         for way, (sign, target) in enumerate(((1, z_down), (-1, z_up))):
-            here = columns_of(partial.at[zmod(z - sign * k), half], way, kind)
-            came = columns_of(sums.at[way, half, min(k, 3)], way, kind)
+            here = columns_of(piece(partial, zmod(z - sign * k), half), way, kind)
+            came = columns_of(piece(sums.at[way], min(k, 3), half), way, kind)
             if k == 2:
                 for i, other in enumerate(("far", "near")):
-                    landed(columns_of(sums.at[way, half, 2], way, other), back_recv.at[way, half, 2, i])
+                    landed(columns_of(piece(sums.at[way], 2, half), way, other), back_recv.at[way, half, 2, i])
             elif k == 1 or (k == 3 and kind == "far"):
                 landed(came, back_recv.at[way, half, k, 0])
             if k < 3 or (k == 3 and kind == "far"):
                 here[...] = (here[...].astype(F32) + came[...].astype(F32)).astype(BF16)
             send(
-                here, columns_of(sums.at[way, half, k - 1], way, kind), back_send.at[way, step],
+                here, columns_of(piece(sums.at[way], k - 1, half), way, kind), back_send.at[way, step],
                 back_recv.at[way, half, k - 1, 1 if kind == "near" else 0], target,
             )
 
@@ -364,8 +386,9 @@
         if slot == 5:
             back_step(0)
         expert_slot(slot)
-        if slot == 0:
+        if slot == 1:
             load_router.wait()
+            lax.fori_loop(0, rows // 64, norm_in, 0)
             logits = jnp.dot(normed[...], router[...], preferred_element_type=F32)
             lane = lax.broadcasted_iota(jnp.int32, logits.shape, 1)
             pick_a = jnp.sum(jnp.where(lane == ids[:, 0:1], logits, 0.0), axis=1, keepdims=True)
@@ -373,17 +396,6 @@
             gate_ref[...] = jnp.where(live[:, 0:1], jax.nn.sigmoid(pick_a - pick_b), 0.0) + jnp.where(
                 live[:, 1:2], jax.nn.sigmoid(pick_b - pick_a), 0.0
             )
-        if slot == 1:
-            token_iota = lax.broadcasted_iota(jnp.int32, (rows, E * 16), 1)
-            for half in range(2):
-                for q in range(4):
-                    put[half, q] = one_hot(token_iota == columns[:, 4 + half:5 + half] + 4 * q)
-        if slot == 2:
-            b_iota = lax.broadcasted_iota(jnp.int32, (E * 16, HALF), 0)
-            s_iota = lax.broadcasted_iota(jnp.int32, (E * 16, HALF), 1)
-            origin = (s_iota // TRIO) * 16 + s_iota % TRIO
-            for q in range(4):
-                unfold[q] = one_hot(b_iota == origin + 4 * q)
         if slot == 3:
             plane1()
 
@@ -399,48 +411,40 @@
         if step == 6:
             plane3()
 
-    for half in range(2):
+    for half in (1, 0):
         for way in range(2):
-            landed(sums.at[way, half, 0], back_recv.at[way, half, 0, 0])
-        total[...] = (
-            partial[z, half].astype(F32) + sums[0, half, 0].astype(F32) + sums[1, half, 0].astype(F32)
-        ).astype(BF16)
-        got = jnp.zeros((E * 16, quarter), F32)
-        for q in range(4):
-            got = got + jnp.dot(
-                unfold[q], total[:, q * quarter:(q + 1) * quarter], preferred_element_type=F32
-            )
-        returning[half] = got.astype(BF16).reshape(E, 16, quarter)
-        for i, (yy, xx) in enumerate(peers):
-            peer = yy * NX + xx
-            send(
-                returning.at[half, peer], returned.at[half, e], ret_send.at[half, i], ret_recv.at[half, e],
-                peer * NZ + z,
-            )
+            landed(piece(sums.at[way], 0, half), back_recv.at[way, half, 0, 0])
+        for pair in PAIRS[half]:
+            at_rows = slice(pair * PAIR, (pair + 1) * PAIR)
+            total = (
+                partial[z, at_rows].astype(F32) + sums[0, 0, at_rows].astype(F32) + sums[1, 0, at_rows].astype(F32)
+            ).astype(BF16)
+            returning[:, :, pair * eighth:(pair + 1) * eighth] = spread(total)
+        exchange(returning, returned, ret_send, ret_recv, half)
         own_back[half].start()
     plane4(0)
-    for half in range(2):
+    gate = gate_ref[...]
+    for half in (1, 0):
+        put = one_hot(
+            lax.broadcasted_iota(jnp.int32, (rows, SIZE[half]), 1) + START[half] == spot_ref[...]
+        )
         own_back[half].wait()
-        for yy, xx in peers:
-            peer = yy * NX + xx
-            landed(returned.at[half, peer], ret_recv.at[half, peer])
-        gate = gate_ref[...]
-        for q in range(4):
-            for j in range(quarter // 256):
-                got = jnp.dot(
-                    put[half, q], returned[half, :, :, j * 256:(j + 1) * 256].reshape(E * 16, 256),
-                    preferred_element_type=F32,
-                )
-                c = q * quarter + j * 256
-                before = mixed[:, c:c + 256] if half else hid[:, c:c + 256].astype(F32)
-                mixed[:, c:c + 256] = before + got * gate
+        exchanged(returned, ret_recv, half)
+        for i, pair in enumerate(PAIRS[half]):
+            back_rows[half, i * PAIR:(i + 1) * PAIR, :] = gathered(returned, pair).astype(BF16)
+        for j in range(width // 256):
+            cols = slice(j * 256, (j + 1) * 256)
+            got = jnp.dot(put, back_rows[half, :SIZE[half], cols], preferred_element_type=F32)
+            before = hid[:, cols].astype(F32) if half else mixed[:, cols]
+            mixed[:, cols] = before + got * gate
 
     def norm_out(i, carry):
-        at_rows = pl.ds(pl.multiple_of(i * 32, 32), 32)
-        normed[at_rows, :] = norm_rows(mixed[at_rows, :], final_gain[...]).astype(BF16)
+        for j in range(4):
+            at_rows = pl.ds(pl.multiple_of(i * 64 + j * 16, 16), 16)
+            normed[at_rows, :] = norm_rows(mixed[at_rows, :], final_gain[...]).astype(BF16)
         return carry
 
-    lax.fori_loop(0, rows // 32, norm_out, 0)
+    lax.fori_loop(0, rows // 64, norm_out, 0)
     plane4(1)
 
     groups = hw // 256
@@ -534,15 +538,14 @@
             pltpu.VMEM((width, 128), BF16),
             pltpu.VMEM((width, ff), BF16),
             pltpu.VMEM((ff, width), BF16),
-            pltpu.VMEM((2, E, 16, width // 4), BF16),
-            pltpu.VMEM((2, E, 16, width // 4), BF16),
-            pltpu.VMEM((NZ, 2, HALF, width), BF16),
-            pltpu.VMEM((NZ, 2, HALF, width), BF16),
-            pltpu.VMEM((2, 2, 4, HALF, width), BF16),
-            pltpu.VMEM((2 * HALF, ff), BF16),
-            pltpu.VMEM((HALF, width), BF16),
-            pltpu.VMEM((2, E, 16, width // 4), BF16),
-            pltpu.VMEM((2, E, 16, width // 4), BF16),
+            pltpu.VMEM((E, 16, 3 * width // 8), BF16),
+            pltpu.VMEM((E, 16, 3 * width // 8), BF16),
+            pltpu.VMEM((NZ, E * C, width), BF16),
+            pltpu.VMEM((NZ, E * C, width), BF16),
+            pltpu.VMEM((2, 4, E * C, width), BF16),
+            pltpu.VMEM((4 * PAIR, ff), BF16),
+            pltpu.VMEM((E, 16, 3 * width // 8), BF16),
+            pltpu.VMEM((E, 16, 3 * width // 8), BF16),
             pltpu.VMEM((rows, width), F32),
             pltpu.VMEM((2, E, NZ, 16, hw), BF16),
             pltpu.VMEM((hw // 256, 2, rows, 256), BF16),
@@ -550,10 +553,11 @@
             pltpu.VMEM((hw // 256, ROWS_Q, 256), BF16),
             pltpu.VMEM((ROWS_Q, hw), BF16),
             pltpu.VMEM((rows, 1), F32),
-            pltpu.VMEM((2, 4, E * 16, rows), BF16),
-            pltpu.VMEM((2, 4, rows, E * 16), BF16),
-            pltpu.VMEM((4, HALF, E * 16), BF16),
-            pltpu.VMEM((4, E * 16, HALF), BF16),
+            pltpu.VMEM((rows, 1), jnp.int32),
+            pltpu.VMEM((E * C, rows), BF16),
+            pltpu.VMEM((E * 16, E * 16), BF16),
+            pltpu.VMEM((E * 16, E * 16), BF16),
+            pltpu.VMEM((2, 2 * PAIR, width), BF16),
             dma((10,)),
             dma((2, 15)),
             dma((2, E)),

time: 101 us -> 100 us (0.990)
  no operation moved by 1% of the time
where the time goes in v3:
time: 100 us
  Pallas kernels  99.2 us (99%)
    pallas_call x1, Pallas kernels, body(): pl.pallas_call(kernel, out_shape=pltpu.VMEM((rows, width), BF16), in_spec...  99.2 us

profile of v3, /device:TPU:1, one launch (start us, length us, event | category | flops | bytes accessed | tf_op | source)
XLA Modules:
  0.0 100.2 jit_solution(8028400217617998645)
XLA Ops:
  0.0 99.2 %shard_map.136 = bf16[256,2048]{1,0:T(8,128)(2,1)S(1)} custom-call(bf16[256,2048]{1,0:T(8,128)(2,1)} %bitcast.14, f32[1,2048]{1,0:T(1,128)} %norm_gain.1, f32[1,2048]{1,0:T(1,128)} %final_gain.1, bf16[2048,128]{1,0:T(8,128)(2,1)} %bitcast.15, bf16[2048,1024]{1,0:T(8,128)(2,1)} %bitcast.12, bf16[1024,2048]{1,0:T(8,128)(2,1)} %bitcast.13, s32[2,256]{1,0:T(2,128)} %bitcast.16, ...), custom_call_target="tpu_custom_call" | custom-call | flops 10000000000 | bytes 12000000 | tf_op jit(solution)/shard_map/pallas_call | solution.py:530
  99.2 1.0 copy.16

commit v4 on v3

--- a/solution.py
+++ b/solution.py
@@ -267,8 +267,8 @@
                 row += SIZE[half]
             return carry
 
-        lax.fori_loop(0, w_in.shape[1] // 256, first_step, 0)
-        lax.fori_loop(0, width // 256, second_step, 0)
+        lax.fori_loop(0, w_in.shape[1] // 256, first_step, 0, unroll=True)
+        lax.fori_loop(0, width // 256, second_step, 0, unroll=True)
 
     def expert_slot(slot):
         half, k = RING[slot]
@@ -444,7 +444,7 @@
             normed[at_rows, :] = norm_rows(mixed[at_rows, :], final_gain[...]).astype(BF16)
         return carry
 
-    lax.fori_loop(0, rows // 64, norm_out, 0)
+    lax.fori_loop(0, rows // 64, norm_out, 0, unroll=True)
     plane4(1)
 
     groups = hw // 256

time: 100 us -> 98.1 us (0.981)
  Pallas kernels: 99.2 us -> 97 us
    pallas_call x1, Pallas kernels: 99.2 us -> 97 us  [body(): pl.pallas_call(kernel, out_shape=pltpu.VMEM((rows, width), BF16), in_spec...]
where the time goes in v4:
time: 98.1 us; the launch traced here: 98 us
  Pallas kernels  97 us (99%)
    pallas_call x1, Pallas kernels, body(): pl.pallas_call(kernel, out_shape=pltpu.VMEM((rows, width), BF16), in_spec...  97 us

profile of v4, /device:TPU:1, one launch (start us, length us, event | category | flops | bytes accessed | tf_op | source)
XLA Modules:
  0.0 98.0 jit_solution(5518439101037236719)
XLA Ops:
  0.0 97.0 %shard_map.136 = bf16[256,2048]{1,0:T(8,128)(2,1)S(1)} custom-call(bf16[256,2048]{1,0:T(8,128)(2,1)} %bitcast.14, f32[1,2048]{1,0:T(1,128)} %norm_gain.1, f32[1,2048]{1,0:T(1,128)} %final_gain.1, bf16[2048,128]{1,0:T(8,128)(2,1)} %bitcast.15, bf16[2048,1024]{1,0:T(8,128)(2,1)} %bitcast.12, bf16[1024,2048]{1,0:T(8,128)(2,1)} %bitcast.13, s32[2,256]{1,0:T(2,128)} %bitcast.16, ...), custom_call_target="tpu_custom_call" | custom-call | flops 10000000000 | bytes 12000000 | tf_op jit(solution)/shard_map/pallas_call | solution.py:530
  97.0 1.0 copy.16
